TPU v7x, 32 devices: a whole 2x2x4 slice. The times are simulated.
32 devices in a mesh: dp: 4 (over x, core), tensor: 8 (over z, y).
Axes of the slice: x: 2, y: 2, z: 4, core: 2. Of those that a mesh axis runs over, the one named last changes fastest.
Arguments:
- tokens: bfloat16 [2, 12288, 1024], P(None, ('dp', 'tensor')), may hold values from -6 to 6
- segment_ids: int32 [2, 4, 3072], P(None, 'dp'), may hold values from 0 to 3, never falling along the last dimension, each value on 1 to 1370 neighbouring positions
- out_grad: bfloat16 [2, 12288, 1024], P(None, ('dp', 'tensor')), may hold values from -6 to 6
- norm1_gain: bfloat16 [1024], P('dp'), may hold values from 0.25 to 1.75
- norm1_bias: bfloat16 [1024], P('dp'), may hold values from -3 to 3
- qkv_weight: bfloat16 [3, 1024, 1024], P(None, 'dp', 'tensor'), may hold values from -0.25 to 0.25
- qv_bias: bfloat16 [2, 1024], P(None, ('tensor', 'dp')), may hold values from -3 to 3
- proj_weight: bfloat16 [1024, 1024], P('tensor', 'dp'), may hold values from -1 to 1
- proj_bias: bfloat16 [1024], P('dp'), may hold values from -3 to 3
- scale1: bfloat16 [1024], P('dp'), may hold values from 0.25 to 1.75
- norm2_gain: bfloat16 [1024], P('dp'), may hold values from 0.25 to 1.75
- norm2_bias: bfloat16 [1024], P('dp'), may hold values from -3 to 3
- fc1_weight: bfloat16 [1024, 4096], P('dp', 'tensor'), may hold values from -0.1875 to 0.1875
- fc1_bias: bfloat16 [4096], P(('tensor', 'dp')), may hold values from -3 to 3
- fc2_weight: bfloat16 [4096, 1024], P('tensor', 'dp'), may hold values from -0.09375 to 0.09375
- fc2_bias: bfloat16 [1024], P('dp'), may hold values from -3 to 3
- scale2: bfloat16 [1024], P('dp'), may hold values from 0.25 to 1.75
Outputs:
- block_out: bfloat16 [2, 12288, 1024], P(None, ('dp', 'tensor'))
- tokens_grad: bfloat16 [2, 12288, 1024], P(None, ('dp', 'tensor'))
- grad_norm1_gain: float32 [1024], P('dp')
- grad_norm1_bias: float32 [1024], P('dp')
- grad_qkv_weight: float32 [3, 1024, 1024], P(None, 'dp', 'tensor')
- grad_qv_bias: float32 [2, 1024], P(None, ('tensor', 'dp'))
- grad_proj_weight: float32 [1024, 1024], P('tensor', 'dp')
- grad_proj_bias: float32 [1024], P('dp')
- grad_scale1: float32 [1024], P('dp')
- grad_norm2_gain: float32 [1024], P('dp')
- grad_norm2_bias: float32 [1024], P('dp')
- grad_fc1_weight: float32 [1024, 4096], P('dp', 'tensor')
- grad_fc1_bias: float32 [4096], P(('tensor', 'dp'))
- grad_fc2_weight: float32 [4096, 1024], P('tensor', 'dp')
- grad_fc2_bias: float32 [1024], P('dp')
- grad_scale2: float32 [1024], P('dp')
Inputs may be any that keep to these rules, and one draw needn't show every extreme that they name: `segment_ids`: along each run the image number never falls; each image is a run of 1 to 1370 tokens, and some image has exactly 1370.
All inputs are finite; a program needn't handle non-finite values.
Results may differ from a plain program's by a relative error of at most 0.023.
Values may be sent and summed in bfloat16 or wider, within the bound.
A program may use at most 192 MiB of HBM per device.

v0:
```python
import jax
import jax.numpy as jnp
from jax import lax
from jax.sharding import PartitionSpec as P

HEAD_DIM = 64


norm_eps = 1e-06
mask_fill = -1e30
contract_rows = (((0,), (0,)), ((), ()))
contract_cols = (((1,), (1,)), ((), ()))


def layer_norm(values, scale_gain, shift_bias):
    center = values - jnp.mean(values, axis=-1, keepdims=True)
    spread = jnp.mean(center * center, axis=-1, keepdims=True)
    return center * lax.rsqrt(spread + norm_eps) * scale_gain + shift_bias


def gelu_exact(values):
    return jax.nn.gelu(values, approximate=False)


def fetch_weights(pieces):
    return (
        lax.all_gather(pieces[0], "dp", axis=1, tiled=True),
        lax.all_gather(pieces[1], "dp", axis=1, tiled=True),
        lax.all_gather(pieces[2], "dp", axis=1, tiled=True),
        lax.all_gather(pieces[3], "dp", axis=0, tiled=True),
        lax.all_gather(pieces[4], "dp", axis=0, tiled=True),
        lax.all_gather(pieces[5], "dp", axis=1, tiled=True),
        lax.all_gather(pieces[6], "dp", axis=1, tiled=True),
    )


def fetch_mlp(gathered):
    return (gathered[3], gathered[4], gathered[5])


def share_grads(local_grads):
    summed = (
        lax.psum_scatter(
            local_grads[0].astype(jnp.bfloat16), "dp", scatter_dimension=1, tiled=True
        ).astype(jnp.float32),
        lax.psum_scatter(
            local_grads[1].astype(jnp.bfloat16), "dp", scatter_dimension=1, tiled=True
        ).astype(jnp.float32),
        lax.psum_scatter(
            local_grads[2].astype(jnp.bfloat16), "dp", scatter_dimension=1, tiled=True
        ).astype(jnp.float32),
        lax.psum_scatter(
            local_grads[3].astype(jnp.bfloat16), "dp", scatter_dimension=0, tiled=True
        ).astype(jnp.float32),
        lax.psum_scatter(
            local_grads[4].astype(jnp.bfloat16), "dp", scatter_dimension=0, tiled=True
        ).astype(jnp.float32),
        lax.psum_scatter(
            local_grads[5].astype(jnp.bfloat16), "dp", scatter_dimension=1, tiled=True
        ).astype(jnp.float32),
        lax.psum_scatter(
            local_grads[6].astype(jnp.bfloat16), "dp", scatter_dimension=1, tiled=True
        ).astype(jnp.float32),
    )
    vector_part = lax.psum(summed[6], "tensor")
    return (summed[0], summed[1], summed[2], summed[3], summed[4], summed[5], vector_part)


def body(
    tokens,
    segment_ids,
    out_grad,
    norm1_gain,
    norm1_bias,
    qkv_weight,
    qv_bias,
    proj_weight,
    proj_bias,
    scale1,
    norm2_gain,
    norm2_bias,
    fc1_weight,
    fc1_bias,
    fc2_weight,
    fc2_bias,
    scale2,
):
    tensor_count = lax.axis_size("tensor")
    rows_here = tokens.shape[1]
    feature_count = tokens.shape[2]
    tok_count = rows_here * tensor_count
    block_rows = min(512, tok_count)
    block_count = tok_count // block_rows
    cols_here = qkv_weight.shape[2]
    heads_here = cols_here // HEAD_DIM
    hidden_here = fc1_weight.shape[1]
    vectors = jnp.stack(
        [norm1_gain, norm1_bias, proj_bias, scale1, norm2_gain, norm2_bias, fc2_bias, scale2]
    )
    pieces = (qkv_weight, qv_bias, proj_weight, fc1_weight, fc1_bias, fc2_weight, vectors)

    def block_scores(query_heads, key_heads, run_ids, row_start):
        query_block = lax.dynamic_slice_in_dim(query_heads, row_start, block_rows, 0)
        ids_query = lax.dynamic_slice_in_dim(run_ids, row_start, block_rows, 0)
        same_image = ids_query[:, None] == run_ids[None, :]
        scores = jnp.einsum(
            "qhd,khd->hqk", query_block, key_heads, preferred_element_type=jnp.float32
        )
        return (query_block, jnp.where(same_image[None], scores, mask_fill))

    def micro_step(carry, inputs):
        tok_rows, seg_row, grad_rows = inputs
        run_ids = seg_row[0]
        gathered = fetch_weights(pieces)
        front_mlp = fetch_mlp(gathered)
        w_qkv = gathered[0]
        bias_qv = gathered[1].astype(jnp.float32)
        w_proj = gathered[2]
        w_fc1 = front_mlp[0]
        bias_fc1 = front_mlp[1].astype(jnp.float32)
        w_fc2 = front_mlp[2]
        vecs = gathered[6].astype(jnp.float32)
        rows_in = tok_rows.astype(jnp.float32)
        normed_one, norm1_pull = jax.vjp(layer_norm, rows_in, vecs[0], vecs[1])
        normed_all = lax.all_gather(normed_one.astype(jnp.bfloat16), "tensor", axis=0, tiled=True)
        projected = jnp.einsum("td,kdc->tkc", normed_all, w_qkv, preferred_element_type=jnp.float32)
        query_rows = ((projected[:, 0] + bias_qv[0]) * 0.125).astype(jnp.bfloat16)
        key_rows = projected[:, 1].astype(jnp.bfloat16)
        value_rows = (projected[:, 2] + bias_qv[1]).astype(jnp.bfloat16)
        query_heads = query_rows.reshape(tok_count, heads_here, HEAD_DIM)
        key_heads = key_rows.reshape(tok_count, heads_here, HEAD_DIM)
        value_heads = value_rows.reshape(tok_count, heads_here, HEAD_DIM)

        def attend(block_id):
            row_start = block_id * block_rows
            _, scores = block_scores(query_heads, key_heads, run_ids, row_start)
            row_top = jnp.max(scores, axis=-1, keepdims=True)
            expon = jnp.exp(scores - row_top)
            row_total = jnp.sum(expon, axis=-1, keepdims=True)
            probs_low = (expon / row_total).astype(jnp.bfloat16)
            block_out = jnp.einsum(
                "hqk,khd->qhd", probs_low, value_heads, preferred_element_type=jnp.float32
            )
            return (block_out, (row_top + jnp.log(row_total))[..., 0])

        attended, log_total = lax.map(attend, jnp.arange(block_count, dtype=jnp.int32))
        attended_low = attended.reshape(tok_count, cols_here).astype(jnp.bfloat16)
        branch_one = (
            lax.psum_scatter(
                jnp.dot(attended_low, w_proj, preferred_element_type=jnp.float32).astype(
                    jnp.bfloat16
                ),
                "tensor",
                scatter_dimension=0,
                tiled=True,
            ).astype(jnp.float32)
            + vecs[2]
        )
        middle = rows_in + vecs[3] * branch_one
        normed_two, norm2_pull = jax.vjp(layer_norm, middle, vecs[4], vecs[5])
        mlp_in = lax.all_gather(normed_two.astype(jnp.bfloat16), "tensor", axis=0, tiled=True)
        pre_act = jnp.dot(mlp_in, w_fc1, preferred_element_type=jnp.float32) + bias_fc1
        activated, gelu_pull = jax.vjp(gelu_exact, pre_act)
        activated_low = activated.astype(jnp.bfloat16)
        branch_two = (
            lax.psum_scatter(
                jnp.dot(activated_low, w_fc2, preferred_element_type=jnp.float32).astype(
                    jnp.bfloat16
                ),
                "tensor",
                scatter_dimension=0,
                tiled=True,
            ).astype(jnp.float32)
            + vecs[6]
        )
        result_rows = (middle + vecs[7] * branch_two).astype(jnp.bfloat16)
        back_weights = fetch_weights(pieces)
        back_mlp = fetch_mlp(back_weights)
        back_qkv = back_weights[0]
        back_proj = back_weights[2]
        back_fc1 = back_mlp[0]
        back_fc2 = back_mlp[2]
        grad_top = grad_rows.astype(jnp.float32)
        d_scale2 = jnp.sum(grad_top * branch_two, axis=0)
        d_branch2 = (vecs[7] * grad_top).astype(jnp.bfloat16)
        d_fc2_bias = jnp.sum(d_branch2.astype(jnp.float32), axis=0)
        d_branch2_all = lax.all_gather(d_branch2, "tensor", axis=0, tiled=True)
        d_fc2 = lax.dot_general(
            activated_low, d_branch2_all, contract_rows, preferred_element_type=jnp.float32
        )
        d_act = lax.dot_general(
            d_branch2_all, back_fc2, contract_cols, preferred_element_type=jnp.float32
        )
        d_pre = gelu_pull(d_act)[0].astype(jnp.bfloat16)
        d_fc1_bias = jnp.sum(d_pre.astype(jnp.float32), axis=0)
        d_fc1 = lax.dot_general(mlp_in, d_pre, contract_rows, preferred_element_type=jnp.float32)
        d_normed_two = lax.psum_scatter(
            lax.dot_general(
                d_pre, back_fc1, contract_cols, preferred_element_type=jnp.float32
            ).astype(jnp.bfloat16),
            "tensor",
            scatter_dimension=0,
            tiled=True,
        ).astype(jnp.float32)
        d_mid_norm, d_gain2, d_bias2 = norm2_pull(d_normed_two)
        d_middle = grad_top + d_mid_norm
        d_scale1 = jnp.sum(d_middle * branch_one, axis=0)
        d_branch1 = (vecs[3] * d_middle).astype(jnp.bfloat16)
        d_proj_bias = jnp.sum(d_branch1.astype(jnp.float32), axis=0)
        d_branch1_all = lax.all_gather(d_branch1, "tensor", axis=0, tiled=True)
        d_proj = lax.dot_general(
            attended_low, d_branch1_all, contract_rows, preferred_element_type=jnp.float32
        )
        d_attended = lax.dot_general(
            d_branch1_all, back_proj, contract_cols, preferred_element_type=jnp.float32
        ).astype(jnp.bfloat16)
        d_att_heads = d_attended.reshape(tok_count, heads_here, HEAD_DIM)

        def attend_back(accum, block_inputs):
            block_id, block_total = block_inputs
            key_accum, value_accum = accum
            row_start = block_id * block_rows
            query_block, scores = block_scores(query_heads, key_heads, run_ids, row_start)
            probs = jnp.exp(scores - block_total[:, :, None])
            probs_low = probs.astype(jnp.bfloat16)
            d_block = lax.dynamic_slice_in_dim(d_att_heads, row_start, block_rows, 0)
            d_probs = jnp.einsum(
                "qhd,khd->hqk", d_block, value_heads, preferred_element_type=jnp.float32
            )
            inner = jnp.sum(probs * d_probs, axis=-1, keepdims=True)
            d_scores = (probs * (d_probs - inner)).astype(jnp.bfloat16)
            d_query = jnp.einsum(
                "hqk,khd->qhd", d_scores, key_heads, preferred_element_type=jnp.float32
            )
            d_key = jnp.einsum(
                "hqk,qhd->khd", d_scores, query_block, preferred_element_type=jnp.float32
            )
            d_value = jnp.einsum(
                "hqk,qhd->khd", probs_low, d_block, preferred_element_type=jnp.float32
            )
            return ((key_accum + d_key, value_accum + d_value), d_query)

        empty_heads = jnp.zeros((tok_count, heads_here, HEAD_DIM), jnp.float32)
        (d_key_sum, d_value_sum), d_query_blocks = lax.scan(
            attend_back,
            (empty_heads, empty_heads),
            (jnp.arange(block_count, dtype=jnp.int32), log_total),
        )
        d_key_low = d_key_sum.reshape(tok_count, cols_here).astype(jnp.bfloat16)
        d_value_low = d_value_sum.reshape(tok_count, cols_here).astype(jnp.bfloat16)
        d_query_low = (d_query_blocks.reshape(tok_count, cols_here) * 0.125).astype(jnp.bfloat16)
        d_qkv = jnp.stack([d_query_low, d_key_low, d_value_low], axis=1)
        d_qkv_weight = jnp.einsum(
            "td,tkc->kdc", normed_all, d_qkv, preferred_element_type=jnp.float32
        )
        d_qv_bias = jnp.stack(
            [
                jnp.sum(d_query_low.astype(jnp.float32), axis=0),
                jnp.sum(d_value_low.astype(jnp.float32), axis=0),
            ]
        )
        d_normed_one = lax.psum_scatter(
            jnp.einsum("tkc,kdc->td", d_qkv, back_qkv, preferred_element_type=jnp.float32).astype(
                jnp.bfloat16
            ),
            "tensor",
            scatter_dimension=0,
            tiled=True,
        ).astype(jnp.float32)
        d_rows_norm, d_gain1, d_bias1 = norm1_pull(d_normed_one)
        input_grad = (d_middle + d_rows_norm).astype(jnp.bfloat16)
        vector_grads = jnp.stack(
            [d_gain1, d_bias1, d_proj_bias, d_scale1, d_gain2, d_bias2, d_fc2_bias, d_scale2]
        )
        local_grads = (d_qkv_weight, d_qv_bias, d_proj, d_fc1, d_fc1_bias, d_fc2, vector_grads)
        new_carry = tuple((old_part + new_part for old_part, new_part in zip(carry, local_grads)))
        return (new_carry, (result_rows, input_grad))

    start_carry = (
        jnp.zeros((3, feature_count, cols_here), jnp.float32),
        jnp.zeros((2, cols_here), jnp.float32),
        jnp.zeros((cols_here, feature_count), jnp.float32),
        jnp.zeros((feature_count, hidden_here), jnp.float32),
        jnp.zeros((hidden_here,), jnp.float32),
        jnp.zeros((hidden_here, feature_count), jnp.float32),
        jnp.zeros((8, feature_count), jnp.float32),
    )
    final_carry, (block_out, tokens_grad) = lax.scan(
        micro_step, start_carry, (tokens, segment_ids, out_grad)
    )
    shards = share_grads(final_carry)
    vec_shards = shards[6]
    return (
        block_out,
        tokens_grad,
        vec_shards[0],
        vec_shards[1],
        shards[0],
        shards[1],
        shards[2],
        vec_shards[2],
        vec_shards[3],
        vec_shards[4],
        vec_shards[5],
        shards[3],
        shards[4],
        shards[5],
        vec_shards[6],
        vec_shards[7],
    )


def solution(mesh):
    in_specs = (
        P(None, ("dp", "tensor"), None),
        P(None, "dp", None),
        P(None, ("dp", "tensor"), None),
        P("dp"),
        P("dp"),
        P(None, "dp", "tensor"),
        P(None, ("tensor", "dp")),
        P("tensor", "dp"),
        P("dp"),
        P("dp"),
        P("dp"),
        P("dp"),
        P("dp", "tensor"),
        P(("tensor", "dp")),
        P("tensor", "dp"),
        P("dp"),
        P("dp"),
    )
    out_specs = (
        P(None, ("dp", "tensor"), None),
        P(None, ("dp", "tensor"), None),
        P("dp"),
        P("dp"),
        P(None, "dp", "tensor"),
        P(None, ("tensor", "dp")),
        P("tensor", "dp"),
        P("dp"),
        P("dp"),
        P("dp"),
        P("dp"),
        P("dp", "tensor"),
        P(("tensor", "dp")),
        P("tensor", "dp"),
        P("dp"),
        P("dp"),
    )
    return jax.shard_map(body, mesh=mesh, in_specs=in_specs, out_specs=out_specs, check_vma=False)
```

profile of v0, /device:TPU:0, one launch (start us, length us, event | category | flops | bytes accessed | tf_op | source)
XLA Modules:
  0.0 2617.1 jit_solution(6725297806182221846)
XLA Ops:
  15.7 2444.1 %while.63 = (s32[]{:T(128)}, f32[3,1024,128]{1,2,0:T(8,128)}, f32[2,128]{1,0:T(2,128)}, f32[128,1024]{1,0:T(8,128)}, f32[1024,512]{1,0:T(8,128)}, /*index=5*/f32...) while((s32[]{:T(128)}, f32[3,1024,128]{1,2,0:T(8,128)}, ...), condition=%wide.region_31.32_spmd.clone.clone, body=%wide.region_0.31_spmd.clone.sunk.clone | while | flops 32089190400 | bytes 696949760 | solution.py:288
  49.0 79.4 %all-gather.17.cloned.1.call-done = bf16[3072,1024]{1,0:T(8,128)(2,1)} async-done(((bf16[384,1024]{1,0:T(8,128)(2,1)}), bf16[3072,1024]{1,0:T(8,128)(2,1)}) %all-gather.17.cloned.1.call-update) | async-done | bytes 6291472 | tf_op jit(solution)/shard_map/while/body/eval_jaxpr/all_gather | solution.py:125
  134.9 78.4 %while.61 = (s32[]{:T(128)}, bf16[6,512,2,64]{1,3,2,0:T(8,128)(2,1)}, f32[6,2,512]{2,1,0:T(2,128)S(1)}, s32[6]{0:T(128)S(1)}, s32[3072]{0:T(1024)S(1)}, /*index=...) while((s32[]{:T(128)}, ...), condition=%wide.region_6.6_spmd, body=%wide.region_3.5_spmd.sunk | while | flops 835189760 | bytes 46057676 | solution.py:146
  222.1 115.1 %reduce-scatter.25.cloned.1.call-done = bf16[384,1024]{1,0:T(8,128)(2,1)} async-done(((bf16[3072,1024]{1,0:T(8,128)(2,1)}), bf16[384,1024]{1,0:T(8,128)(2,1)}) %reduce-scatter.25.cloned.1.call-update) | async-done | bytes 786448 | tf_op jit(solution)/shard_map/while/body/eval_jaxpr/reduce_scatter | solution.py:149
  349.4 89.4 %all-gather.19.cloned.1.call-done = bf16[3072,1024]{1,0:T(8,128)(2,1)} async-done(((bf16[384,1024]{1,0:T(8,128)(2,1)}), bf16[3072,1024]{1,0:T(8,128)(2,1)}) %all-gather.19.cloned.1.call-update) | async-done | bytes 6291472 | tf_op jit(solution)/shard_map/while/body/eval_jaxpr/all_gather | solution.py:161
  459.1 97.0 %all-gather.23.cloned.1.call-done = bf16[3072,1024]{1,0:T(8,128)(2,1)} async-done(((bf16[384,1024]{1,0:T(8,128)(2,1)}), bf16[3072,1024]{1,0:T(8,128)(2,1)}) %all-gather.23.cloned.1.call-update) | async-done | bytes 6291472 | tf_op jit(solution)/shard_map/while/body/eval_jaxpr/all_gather | solution.py:187
  585.3 107.7 %reduce-scatter.27.cloned.1.call-done = bf16[384,1024]{1,0:T(8,128)(2,1)} async-done(((bf16[3072,1024]{1,0:T(8,128)(2,1)}), bf16[384,1024]{1,0:T(8,128)(2,1)}) %reduce-scatter.27.cloned.1.call-update) | async-done | bytes 786448 | tf_op jit(solution)/shard_map/while/body/eval_jaxpr/reduce_scatter | solution.py:197
  697.2 116.4 %reduce-scatter.29.cloned.1.call-done = bf16[384,1024]{1,0:T(8,128)(2,1)} async-done(((bf16[3072,1024]{1,0:T(8,128)(2,1)}), bf16[384,1024]{1,0:T(8,128)(2,1)}) %reduce-scatter.29.cloned.1.call-update) | async-done | bytes 786448 | tf_op jit(solution)/shard_map/while/body/eval_jaxpr/reduce_scatter | solution.py:166
  820.0 97.9 %all-gather.27.cloned.1.call-done = bf16[3072,1024]{1,0:T(8,128)(2,1)} async-done(((bf16[384,1024]{1,0:T(8,128)(2,1)}), bf16[3072,1024]{1,0:T(8,128)(2,1)}) %all-gather.27.cloned.1.call-update) | async-done | bytes 6291472 | tf_op jit(solution)/shard_map/while/body/eval_jaxpr/all_gather | solution.py:210
  923.8 180.6 %while.62 = (s32[]{:T(128)}, f32[3072,2,64]{0,2,1:T(8,128)S(1)}, f32[3072,2,64]{0,2,1:T(8,128)}, f32[6,512,2,64]{1,3,2,0:T(8,128)}, s32[6]{0:T(128)S(1)}, /*inde...) while((s32[]{:T(128)}, f32[3072,2,64]{0,2,1:T(8,128)S(1)}, ...), condition=%wide.region_15.15_spmd.clone, body=%wide.region_13.14_spmd.clone.sunk | while | flops 2054159360 | bytes 122730808 | solution.py:244
  1144.4 87.4 %reduce-scatter.31.cloned.1.call-done = bf16[384,1024]{1,0:T(8,128)(2,1)} async-done(((bf16[3072,1024]{1,0:T(8,128)(2,1)}), bf16[384,1024]{1,0:T(8,128)(2,1)}) %reduce-scatter.31.cloned.1.call-update) | async-done | bytes 786448 | tf_op jit(solution)/shard_map/while/body/eval_jaxpr/reduce_scatter | solution.py:262
  1270.5 77.4 %all-gather.17.cloned.1.call-done = bf16[3072,1024]{1,0:T(8,128)(2,1)} async-done(((bf16[384,1024]{1,0:T(8,128)(2,1)}), bf16[3072,1024]{1,0:T(8,128)(2,1)}) %all-gather.17.cloned.1.call-update) | async-done | bytes 6291472 | tf_op jit(solution)/shard_map/while/body/eval_jaxpr/all_gather | solution.py:125
  1354.4 78.4 %while.61 = (s32[]{:T(128)}, bf16[6,512,2,64]{1,3,2,0:T(8,128)(2,1)}, f32[6,2,512]{2,1,0:T(2,128)S(1)}, s32[6]{0:T(128)S(1)}, s32[3072]{0:T(1024)S(1)}, /*index=...) while((s32[]{:T(128)}, ...), condition=%wide.region_6.6_spmd, body=%wide.region_3.5_spmd.sunk | while | flops 835189760 | bytes 46057676 | solution.py:146
  1441.3 115.4 %reduce-scatter.25.cloned.1.call-done = bf16[384,1024]{1,0:T(8,128)(2,1)} async-done(((bf16[3072,1024]{1,0:T(8,128)(2,1)}), bf16[384,1024]{1,0:T(8,128)(2,1)}) %reduce-scatter.25.cloned.1.call-update) | async-done | bytes 786448 | tf_op jit(solution)/shard_map/while/body/eval_jaxpr/reduce_scatter | solution.py:149
  1568.8 89.4 %all-gather.19.cloned.1.call-done = bf16[3072,1024]{1,0:T(8,128)(2,1)} async-done(((bf16[384,1024]{1,0:T(8,128)(2,1)}), bf16[3072,1024]{1,0:T(8,128)(2,1)}) %all-gather.19.cloned.1.call-update) | async-done | bytes 6291472 | tf_op jit(solution)/shard_map/while/body/eval_jaxpr/all_gather | solution.py:161
  1678.5 97.0 %all-gather.23.cloned.1.call-done = bf16[3072,1024]{1,0:T(8,128)(2,1)} async-done(((bf16[384,1024]{1,0:T(8,128)(2,1)}), bf16[3072,1024]{1,0:T(8,128)(2,1)}) %all-gather.23.cloned.1.call-update) | async-done | bytes 6291472 | tf_op jit(solution)/shard_map/while/body/eval_jaxpr/all_gather | solution.py:187
  1805.0 107.5 %reduce-scatter.27.cloned.1.call-done = bf16[384,1024]{1,0:T(8,128)(2,1)} async-done(((bf16[3072,1024]{1,0:T(8,128)(2,1)}), bf16[384,1024]{1,0:T(8,128)(2,1)}) %reduce-scatter.27.cloned.1.call-update) | async-done | bytes 786448 | tf_op jit(solution)/shard_map/while/body/eval_jaxpr/reduce_scatter | solution.py:197
  1916.6 116.6 %reduce-scatter.29.cloned.1.call-done = bf16[384,1024]{1,0:T(8,128)(2,1)} async-done(((bf16[3072,1024]{1,0:T(8,128)(2,1)}), bf16[384,1024]{1,0:T(8,128)(2,1)}) %reduce-scatter.29.cloned.1.call-update) | async-done | bytes 786448 | tf_op jit(solution)/shard_map/while/body/eval_jaxpr/reduce_scatter | solution.py:166
  2039.6 97.9 %all-gather.27.cloned.1.call-done = bf16[3072,1024]{1,0:T(8,128)(2,1)} async-done(((bf16[384,1024]{1,0:T(8,128)(2,1)}), bf16[3072,1024]{1,0:T(8,128)(2,1)}) %all-gather.27.cloned.1.call-update) | async-done | bytes 6291472 | tf_op jit(solution)/shard_map/while/body/eval_jaxpr/all_gather | solution.py:210
  2143.4 180.5 %while.62 = (s32[]{:T(128)}, f32[3072,2,64]{0,2,1:T(8,128)S(1)}, f32[3072,2,64]{0,2,1:T(8,128)}, f32[6,512,2,64]{1,3,2,0:T(8,128)}, s32[6]{0:T(128)S(1)}, /*inde...) while((s32[]{:T(128)}, f32[3072,2,64]{0,2,1:T(8,128)S(1)}, ...), condition=%wide.region_15.15_spmd.clone, body=%wide.region_13.14_spmd.clone.sunk | while | flops 2054159360 | bytes 122730808 | solution.py:244
  2364.7 86.6 %reduce-scatter.31.cloned.1.call-done = bf16[384,1024]{1,0:T(8,128)(2,1)} async-done(((bf16[3072,1024]{1,0:T(8,128)(2,1)}), bf16[384,1024]{1,0:T(8,128)(2,1)}) %reduce-scatter.31.cloned.1.call-update) | async-done | bytes 786448 | tf_op jit(solution)/shard_map/while/body/eval_jaxpr/reduce_scatter | solution.py:262
  2528.7 24.3 reduce-scatter.15.cloned.1.call-done
  2554.7 25.8 reduce-scatter.19.cloned.1.call-done
  2582.2 25.7 reduce-scatter.21.cloned.1.call-done
  (741 shorter events, 924.9 us)
Async XLA Ops:
  15.7 112.7 %all-gather.17.cloned.1.call-start = ((), (), s32[]{:S(2)}) async-start(), calls=%async_computation.16 | async-start | bytes 7077888 | tf_op jit(solution)/shard_map/while/body/eval_jaxpr/all_gather | solution.py:125
  27.5 309.7 %reduce-scatter.25.cloned.1.call-start = ((), (), s32[]{:S(2)}) async-start(), calls=%async_computation.17 | async-start | bytes 7077888 | tf_op jit(solution)/shard_map/while/body/eval_jaxpr/reduce_scatter | solution.py:149
  221.0 128.4 %all-gather.21.cloned.1.call-start = ((), (), s32[]{:S(2)}) async-start(), calls=%async_computation.19 | async-start | bytes 1310720 | tf_op jit(solution)/shard_map/while/body/eval_jaxpr/all_gather | solution.py:30
  221.6 217.3 %all-gather.19.cloned.1.call-start = ((), (), s32[]{:S(2)}) async-start(), calls=%async_computation.18 | async-start | bytes 7077888 | tf_op jit(solution)/shard_map/while/body/eval_jaxpr/all_gather | solution.py:161
  340.8 118.2 %all-gather.25.cloned.1.call-start = ((), (), s32[]{:S(2)}) async-start(), calls=%async_computation.21 | async-start | bytes 1310720 | tf_op jit(solution)/shard_map/while/body/eval_jaxpr/all_gather | solution.py:32
  341.4 214.7 %all-gather.23.cloned.1.call-start = ((), (), s32[]{:S(2)}) async-start(), calls=%async_computation.20 | async-start | bytes 7077888 | tf_op jit(solution)/shard_map/while/body/eval_jaxpr/all_gather | solution.py:187
  344.3 348.7 %reduce-scatter.27.cloned.1.call-start = ((), (), s32[]{:S(2)}) async-start(), calls=%async_computation.22 | async-start | bytes 7077888 | tf_op jit(solution)/shard_map/while/body/eval_jaxpr/reduce_scatter | solution.py:197
  576.7 236.8 %reduce-scatter.29.cloned.1.call-start = ((), (), s32[]{:S(2)}) async-start(), calls=%async_computation.23 | async-start | bytes 7077888 | tf_op jit(solution)/shard_map/while/body/eval_jaxpr/reduce_scatter | solution.py:166
  585.2 332.7 %all-gather.27.cloned.1.call-start = ((), (), s32[]{:S(2)}) async-start(), calls=%async_computation.24 | async-start | bytes 7077888 | tf_op jit(solution)/shard_map/while/body/eval_jaxpr/all_gather | solution.py:210
  819.9 411.9 %reduce-scatter.31.cloned.1.call-start = ((), (), s32[]{:S(2)}) async-start(), calls=%async_computation.25 | async-start | bytes 7077888 | tf_op jit(solution)/shard_map/while/body/eval_jaxpr/reduce_scatter | solution.py:262
  1238.5 109.3 %all-gather.17.cloned.1.call-start = ((), (), s32[]{:S(2)}) async-start(), calls=%async_computation.16 | async-start | bytes 7077888 | tf_op jit(solution)/shard_map/while/body/eval_jaxpr/all_gather | solution.py:125
  1249.3 307.4 %reduce-scatter.25.cloned.1.call-start = ((), (), s32[]{:S(2)}) async-start(), calls=%async_computation.17 | async-start | bytes 7077888 | tf_op jit(solution)/shard_map/while/body/eval_jaxpr/reduce_scatter | solution.py:149
  1440.4 128.4 %all-gather.21.cloned.1.call-start = ((), (), s32[]{:S(2)}) async-start(), calls=%async_computation.19 | async-start | bytes 1310720 | tf_op jit(solution)/shard_map/while/body/eval_jaxpr/all_gather | solution.py:30
  1441.0 217.2 %all-gather.19.cloned.1.call-start = ((), (), s32[]{:S(2)}) async-start(), calls=%async_computation.18 | async-start | bytes 7077888 | tf_op jit(solution)/shard_map/while/body/eval_jaxpr/all_gather | solution.py:161
  1560.3 118.2 %all-gather.25.cloned.1.call-start = ((), (), s32[]{:S(2)}) async-start(), calls=%async_computation.21 | async-start | bytes 1310720 | tf_op jit(solution)/shard_map/while/body/eval_jaxpr/all_gather | solution.py:32
  1560.8 214.7 %all-gather.23.cloned.1.call-start = ((), (), s32[]{:S(2)}) async-start(), calls=%async_computation.20 | async-start | bytes 7077888 | tf_op jit(solution)/shard_map/while/body/eval_jaxpr/all_gather | solution.py:187
  1563.7 348.7 %reduce-scatter.27.cloned.1.call-start = ((), (), s32[]{:S(2)}) async-start(), calls=%async_computation.22 | async-start | bytes 7077888 | tf_op jit(solution)/shard_map/while/body/eval_jaxpr/reduce_scatter | solution.py:197
  1796.2 237.0 %reduce-scatter.29.cloned.1.call-start = ((), (), s32[]{:S(2)}) async-start(), calls=%async_computation.23 | async-start | bytes 7077888 | tf_op jit(solution)/shard_map/while/body/eval_jaxpr/reduce_scatter | solution.py:166
  1804.9 332.6 %all-gather.27.cloned.1.call-start = ((), (), s32[]{:S(2)}) async-start(), calls=%async_computation.24 | async-start | bytes 7077888 | tf_op jit(solution)/shard_map/while/body/eval_jaxpr/all_gather | solution.py:210
  2039.5 411.8 %reduce-scatter.31.cloned.1.call-start = ((), (), s32[]{:S(2)}) async-start(), calls=%async_computation.25 | async-start | bytes 7077888 | tf_op jit(solution)/shard_map/while/body/eval_jaxpr/reduce_scatter | solution.py:262
  2462.8 64.4 %reduce-scatter.17.cloned.1.call-start = ((), (), s32[]{:S(2)}) async-start(), calls=%async_computation.12 | async-start | bytes 327680 | tf_op jit(solution)/shard_map/reduce_scatter | solution.py:49
  2464.8 88.2 %reduce-scatter.15.cloned.1.call-start = ((), (), s32[]{:S(2)}) async-start(), calls=%async_computation.11 | async-start | bytes 983040 | tf_op jit(solution)/shard_map/reduce_scatter | solution.py:43
  2467.5 113.0 %reduce-scatter.19.cloned.1.call-start = ((), (), s32[]{:S(2)}) async-start(), calls=%async_computation.13 | async-start | bytes 1310720 | tf_op jit(solution)/shard_map/reduce_scatter | solution.py:52
  2468.7 139.2 %reduce-scatter.21.cloned.1.call-start = ((), (), s32[]{:S(2)}) async-start(), calls=%async_computation.14 | async-start | bytes 1310720 | tf_op jit(solution)/shard_map/reduce_scatter | solution.py:58
  (151 other events, 6412.1 us)
Sparse Core Ops, SparseCore 0:
  27.6 100.7 all-gather.16
  221.1 116.1 reduce-scatter.24
  576.8 116.1 reduce-scatter.26
  696.5 117.0 reduce-scatter.28
  1249.4 98.3 all-gather.16
  1440.5 116.1 reduce-scatter.24
  1796.3 116.1 reduce-scatter.26
  1916.0 117.0 reduce-scatter.28
  2463.7 18.5 reduce-scatter.22
  2484.7 19.3 reduce-scatter.12
  2507.1 20.0 reduce-scatter.16
  2529.7 23.2 reduce-scatter.14
  2555.5 24.9 reduce-scatter.18
  2583.0 24.8 reduce-scatter.20
Sparse Core Ops, SparseCore 1:
  223.0 14.8 all-gather.20
  340.9 97.8 all-gather.18
  440.2 14.8 all-gather.24
  457.3 98.7 all-gather.22
  820.0 97.9 all-gather.26
  1116.0 115.8 reduce-scatter.30
  1442.4 14.7 all-gather.20
  1560.3 97.8 all-gather.18
  1659.7 14.8 all-gather.24
  1676.8 98.7 all-gather.22
  2039.6 97.8 all-gather.26
  2335.5 115.7 reduce-scatter.30
where the time goes:
time: 2620 us
  waiting for transfers between devices  1680 us (64%)
  matrix products  518 us (20%)
  other arithmetic  227 us (9%)
  blocking collectives  89.1 us (3%)
  local copies, waits for them, and re-layouts  61.4 us (2%)
    reduce_scatter x2, waiting for transfers between devices, micro_step(): lax.psum_scatter(jnp.dot(activated_low, w_fc2, preferred_element_type=jnp...  233 us
    reduce_scatter x2, waiting for transfers between devices, micro_step(): lax.psum_scatter(jnp.dot(attended_low, w_proj, preferred_element_type=jnp...  231 us
    reduce_scatter x2, waiting for transfers between devices, micro_step(): lax.psum_scatter(lax.dot_general(d_pre, back_fc1, contract_cols, preferre...  215 us
    all_gather x2, waiting for transfers between devices, micro_step(): d_branch1_all = lax.all_gather(d_branch1, 'tensor', axis=0, tiled=True)  196 us
    all_gather x2, waiting for transfers between devices, micro_step(): d_branch2_all = lax.all_gather(d_branch2, 'tensor', axis=0, tiled=True)  194 us
    all_gather x2, waiting for transfers between devices, micro_step(): lax.all_gather(normed_two.astype(jnp.bfloat16), 'tensor', axis=0, tiled=T...  179 us
    reduce_scatter x2, waiting for transfers between devices, micro_step(): lax.psum_scatter(jnp.einsum('tkc,kdc->td', d_qkv, back_qkv, preferred_ele...  174 us
    all_gather x2, waiting for transfers between devices, micro_step(): lax.all_gather(normed_one.astype(jnp.bfloat16), 'tensor', axis=0, tiled=T...  157 us
  transfers between devices with their start and end apart: 26, of which 22 were waited for; matrix products, arithmetic and copies ran while one was open for 6% of the time, Pallas kernels for 0%

commit v1 on v0

v1 whole, which is shorter than its diff:
```python
import jax
import jax.numpy as jnp
from jax import lax
from jax.experimental import pallas as pl
from jax.experimental.pallas import tpu as pltpu
from jax.sharding import PartitionSpec as P

HEAD_DIM = 64

norm_eps = 1e-06
mask_fill = -1e30
query_rows = 512
key_rows = 512
contract_rows = (((0,), (0,)), ((), ()))
contract_cols = (((1,), (1,)), ((), ()))
everywhere = ("dp", "tensor")


def dot_f32(left, right, dims=(((1,), (0,)), ((), ()))):
    return lax.dot_general(left, right, dims, preferred_element_type=jnp.float32)


def norm_parts(values):
    center = values - jnp.mean(values, axis=-1, keepdims=True)
    rate = lax.rsqrt(jnp.mean(center * center, axis=-1, keepdims=True) + norm_eps)
    return center * rate, rate


def norm_back(normed, rate, gain, grad):
    scaled = gain * grad
    average = jnp.mean(scaled, axis=-1, keepdims=True)
    along = jnp.mean(scaled * normed, axis=-1, keepdims=True)
    return rate * (scaled - average - normed * along)


def head_part(rows, head):
    lane = lax.broadcasted_iota(jnp.int32, rows.shape, 1)
    return jnp.where(lane // HEAD_DIM == head, rows, jnp.zeros_like(rows))


def forward_kernel(low_ref, high_ref, q_ref, k_ref, v_ref, idq_ref, idk_ref, out_ref, lse_ref):
    batch, block = pl.program_id(0), pl.program_id(1)
    queries = q_ref[0]
    heads = queries.shape[1] // HEAD_DIM
    rows = queries.shape[0]
    parts = [head_part(queries, head) for head in range(heads)]
    ids_query = idq_ref[0]

    def step(index, carry):
        start = pl.multiple_of(index * key_rows, key_rows)
        keys = k_ref[0, pl.ds(start, key_rows), :]
        values = v_ref[0, pl.ds(start, key_rows), :].T
        same = idk_ref[0, pl.ds(start, key_rows), :] == ids_query
        result = []
        for head in range(heads):
            top, total, acc = carry[head]
            scores = jnp.where(same, dot_f32(keys, parts[head], contract_cols), mask_fill)
            new_top = jnp.maximum(top, jnp.max(scores, axis=0, keepdims=True))
            expon = jnp.exp(scores - new_top)
            shrink = jnp.exp(top - new_top)
            total = shrink * total + jnp.sum(expon, axis=0, keepdims=True)
            mine = values[head * HEAD_DIM : (head + 1) * HEAD_DIM]
            acc = shrink * acc + dot_f32(mine, expon.astype(jnp.bfloat16))
            result.append((new_top, total, acc))
        return tuple(result)

    start_carry = tuple(
        (
            jnp.full((1, rows), mask_fill, jnp.float32),
            jnp.zeros((1, rows), jnp.float32),
            jnp.zeros((HEAD_DIM, rows), jnp.float32),
        )
        for _ in range(heads)
    )
    final = lax.fori_loop(low_ref[batch, block], high_ref[batch, block], step, start_carry)
    merged = jnp.concatenate([acc / total for _, total, acc in final], axis=0)
    out_ref[0] = merged.T.astype(out_ref.dtype)
    lse_ref[0, 0] = jnp.concatenate([top + jnp.log(total) for top, total, _ in final], axis=0)


def backward_kernel(
    low_ref, high_ref, q_ref, k_ref, v_ref, idq_ref, idk_ref, att_ref, d_att_ref, lse_ref,
    dq_ref, dk_ref, dv_ref, dk_sum, dv_sum,
):
    batch, block = pl.program_id(0), pl.program_id(1)

    @pl.when(block == 0)
    def _():
        dk_sum[...] = jnp.zeros_like(dk_sum)
        dv_sum[...] = jnp.zeros_like(dv_sum)

    queries, d_att = q_ref[0], d_att_ref[0]
    heads = queries.shape[1] // HEAD_DIM
    rows = queries.shape[0]
    parts = [head_part(queries, head) for head in range(heads)]
    d_parts = [head_part(d_att, head) for head in range(heads)]
    ids_query = idq_ref[0]
    products = (att_ref[0].astype(jnp.float32) * d_att.astype(jnp.float32)).T
    inner = [
        jnp.sum(products[head * HEAD_DIM : (head + 1) * HEAD_DIM], axis=0, keepdims=True)
        for head in range(heads)
    ]
    lse = lse_ref[0, 0]

    def step(index, carry):
        start = pl.multiple_of(index * key_rows, key_rows)
        here = pl.ds(start, key_rows)
        keys, values = k_ref[0, here, :], v_ref[0, here, :]
        keys_turned = keys.T
        same = idk_ref[0, here, :] == ids_query
        result = []
        d_value, d_key = dv_sum[here, :], dk_sum[here, :]
        for head in range(heads):
            scores = jnp.where(same, dot_f32(keys, parts[head], contract_cols), mask_fill)
            probs = jnp.exp(scores - lse[head : head + 1])
            d_probs = dot_f32(values, d_parts[head], contract_cols)
            d_scores = (probs * (d_probs - inner[head])).astype(jnp.bfloat16)
            d_value = d_value + dot_f32(probs.astype(jnp.bfloat16), d_parts[head])
            d_key = d_key + dot_f32(d_scores, parts[head])
            mine = keys_turned[head * HEAD_DIM : (head + 1) * HEAD_DIM]
            result.append(carry[head] + dot_f32(mine, d_scores))
        dv_sum[here, :] = d_value
        dk_sum[here, :] = d_key
        return tuple(result)

    empty = tuple(jnp.zeros((HEAD_DIM, rows), jnp.float32) for _ in range(heads))
    final = lax.fori_loop(low_ref[batch, block], high_ref[batch, block], step, empty)
    dq_ref[0] = (jnp.concatenate(final, axis=0).T * 0.125).astype(dq_ref.dtype)

    @pl.when(block == pl.num_programs(1) - 1)
    def _():
        dk_ref[0] = dk_sum[...].astype(dk_ref.dtype)
        dv_ref[0] = dv_sum[...].astype(dv_ref.dtype)


def attention_inputs(qkv):
    cols = qkv.shape[2] // 3
    if cols % 128 == 0:
        return qkv, qkv, qkv
    return qkv[..., :cols], qkv[..., cols : 2 * cols], qkv[..., 2 * cols :]


def attention_specs(tok_count, cols):
    spot_k, spot_v = (1, 2) if cols % 128 == 0 else (0, 0)
    q_spec = pl.BlockSpec((1, query_rows, cols), lambda b, i, *_: (b, i, 0))
    k_spec = pl.BlockSpec((1, tok_count, cols), lambda b, i, *_: (b, 0, spot_k))
    v_spec = pl.BlockSpec((1, tok_count, cols), lambda b, i, *_: (b, 0, spot_v))
    whole = pl.BlockSpec((1, tok_count, cols), lambda b, i, *_: (b, 0, 0))
    idq_spec = pl.BlockSpec((1, 1, query_rows), lambda b, i, *_: (b, 0, i))
    idk_spec = pl.BlockSpec((1, tok_count, 1), lambda b, i, *_: (b, 0, 0))
    lse_spec = pl.BlockSpec(
        (1, 1, cols // HEAD_DIM, query_rows), lambda b, i, *_: (b, i, 0, 0)
    )
    return q_spec, k_spec, v_spec, whole, idq_spec, idk_spec, lse_spec


def attention(qkv, bounds, ids_row, ids_col):
    batches, tok_count, cols3 = qkv.shape
    cols = cols3 // 3
    blocks = tok_count // query_rows
    q_spec, k_spec, v_spec, _, idq_spec, idk_spec, lse_spec = attention_specs(
        tok_count, cols
    )
    pairs = batches * tok_count * tok_count // 2
    return pl.pallas_call(
        forward_kernel,
        grid_spec=pltpu.PrefetchScalarGridSpec(
            num_scalar_prefetch=2,
            grid=(batches, blocks),
            in_specs=[q_spec, k_spec, v_spec, idq_spec, idk_spec],
            out_specs=[q_spec, lse_spec],
        ),
        out_shape=[
            jax.ShapeDtypeStruct((batches, tok_count, cols), jnp.bfloat16),
            jax.ShapeDtypeStruct(
                (batches, blocks, cols // HEAD_DIM, query_rows), jnp.float32
            ),
        ],
        compiler_params=pltpu.CompilerParams(vmem_limit_bytes=40 * 1024 * 1024),
        cost_estimate=pl.CostEstimate(
            flops=pairs * 16 * cols, bytes_accessed=2 * qkv.size, transcendentals=2 * pairs
        ),
    )(*bounds, *attention_inputs(qkv), ids_row, ids_col)


def attention_back(qkv, bounds, ids_row, ids_col, att, d_att, lse):
    batches, tok_count, cols3 = qkv.shape
    cols = cols3 // 3
    blocks = tok_count // query_rows
    q_spec, k_spec, v_spec, whole, idq_spec, idk_spec, lse_spec = attention_specs(
        tok_count, cols
    )
    pairs = batches * tok_count * tok_count // 2
    one = jax.ShapeDtypeStruct((batches, tok_count, cols), jnp.bfloat16)
    return pl.pallas_call(
        backward_kernel,
        grid_spec=pltpu.PrefetchScalarGridSpec(
            num_scalar_prefetch=2,
            grid=(batches, blocks),
            in_specs=[q_spec, k_spec, v_spec, idq_spec, idk_spec, q_spec, q_spec, lse_spec],
            out_specs=[q_spec, whole, whole],
            scratch_shapes=[
                pltpu.VMEM((tok_count, cols), jnp.float32),
                pltpu.VMEM((tok_count, cols), jnp.float32),
            ],
        ),
        out_shape=[one, one, one],
        compiler_params=pltpu.CompilerParams(vmem_limit_bytes=48 * 1024 * 1024),
        cost_estimate=pl.CostEstimate(
            flops=pairs * 40 * cols, bytes_accessed=4 * qkv.size, transcendentals=2 * pairs
        ),
    )(*bounds, *attention_inputs(qkv), ids_row, ids_col, att, d_att, lse)


def gather_matrix(shard):
    part = lax.all_gather(shard, "tensor", axis=1, tiled=True)
    return lax.all_gather(part, "dp", axis=0, tiled=True)


def scatter_matrix(grad):
    part = lax.psum_scatter(grad.astype(jnp.bfloat16), "dp", scatter_dimension=0, tiled=True)
    return lax.psum_scatter(part, "tensor", scatter_dimension=1, tiled=True).astype(jnp.float32)


def body(
    tokens,
    segment_ids,
    out_grad,
    norm1_gain,
    norm1_bias,
    qkv_weight,
    qv_bias,
    proj_weight,
    proj_bias,
    scale1,
    norm2_gain,
    norm2_bias,
    fc1_weight,
    fc1_bias,
    fc2_weight,
    fc2_bias,
    scale2,
):
    tensor_count = lax.axis_size("tensor")
    dp_count = lax.axis_size("dp")
    batches, rows_here, width = tokens.shape
    total_rows = batches * rows_here
    tok_count = rows_here * tensor_count
    cols_here = qkv_weight.shape[2]
    shard_rows = qkv_weight.shape[1]
    hidden = fc1_weight.shape[1] * tensor_count

    vectors = jnp.stack(
        [norm1_gain, norm1_bias, proj_bias, scale1, norm2_gain, norm2_bias, fc2_bias, scale2]
    )
    vecs = lax.all_gather(vectors, "dp", axis=1, tiled=True).astype(jnp.float32)
    short = qv_bias.shape[1]
    biases = jnp.concatenate([qv_bias.reshape(-1), fc1_bias])
    biases = lax.all_gather(biases, ("tensor", "dp"), axis=0, tiled=False).astype(jnp.float32)
    bias_q = biases[:, :short].reshape(tensor_count, 1, cols_here)
    bias_v = biases[:, short : 2 * short].reshape(tensor_count, 1, cols_here)
    bias_fc1 = biases[:, 2 * short :].reshape(hidden)
    bias_qkv = jnp.concatenate([bias_q, jnp.zeros_like(bias_q), bias_v], axis=1).reshape(-1)
    scale_qkv = jnp.concatenate(
        [jnp.full_like(bias_q, 0.125), jnp.ones_like(bias_q), jnp.ones_like(bias_q)], axis=1
    ).reshape(-1)

    w_qkv = gather_matrix(jnp.moveaxis(qkv_weight, 0, 1).reshape(shard_rows, 3 * cols_here))
    w_proj = gather_matrix(proj_weight.T)
    w_fc1 = gather_matrix(fc1_weight)
    w_fc2 = gather_matrix(fc2_weight.T)

    run_ids = segment_ids[:, 0]
    blocks = tok_count // query_rows
    first = run_ids.reshape(batches, blocks, query_rows)[:, :, :1]
    last = run_ids.reshape(batches, blocks, query_rows)[:, :, -1:]
    low = jnp.sum((run_ids[:, None, :] < first).astype(jnp.int32), axis=-1) // key_rows
    reach = jnp.sum((run_ids[:, None, :] <= last).astype(jnp.int32), axis=-1)
    bounds = (low, (reach + key_rows - 1) // key_rows)
    ids_row, ids_col = run_ids[:, None, :], run_ids[:, :, None]

    rows_in = tokens.reshape(total_rows, width).astype(jnp.float32)
    normed_one, rate_one = norm_parts(rows_in)
    normed_one_low = (normed_one * vecs[0] + vecs[1]).astype(jnp.bfloat16)
    projected = ((dot_f32(normed_one_low, w_qkv) + bias_qkv) * scale_qkv).astype(jnp.bfloat16)
    qkv = lax.all_to_all(
        projected.reshape(batches, rows_here, tensor_count * 3 * cols_here),
        "tensor", split_axis=2, concat_axis=1, tiled=True,
    )
    att_heads, lse = attention(qkv, bounds, ids_row, ids_col)
    attended = lax.all_to_all(
        att_heads, "tensor", split_axis=1, concat_axis=2, tiled=True
    ).reshape(total_rows, width)
    branch_one = dot_f32(attended, w_proj, contract_cols) + vecs[2]
    middle = rows_in + vecs[3] * branch_one
    normed_two, rate_two = norm_parts(middle)
    mlp_in = (normed_two * vecs[4] + vecs[5]).astype(jnp.bfloat16)
    pre_act = dot_f32(mlp_in, w_fc1) + bias_fc1
    spread = 0.5 * (1.0 + lax.erf(pre_act * 0.7071067811865476))
    activated = (pre_act * spread).astype(jnp.bfloat16)
    slope = spread + pre_act * jnp.exp(-0.5 * pre_act * pre_act) * 0.3989422804014327
    branch_two = dot_f32(activated, w_fc2, contract_cols) + vecs[6]
    block_out = (middle + vecs[7] * branch_two).astype(jnp.bfloat16)

    grad_top = out_grad.reshape(total_rows, width).astype(jnp.float32)
    d_scale2 = jnp.sum(grad_top * branch_two, axis=0)
    d_branch2 = (vecs[7] * grad_top).astype(jnp.bfloat16)
    d_fc2_bias = jnp.sum(d_branch2.astype(jnp.float32), axis=0)
    d_fc2 = dot_f32(d_branch2, activated, contract_rows)
    d_pre = (dot_f32(d_branch2, w_fc2) * slope).astype(jnp.bfloat16)
    d_fc1_bias = jnp.sum(d_pre.astype(jnp.float32), axis=0)
    d_fc1 = dot_f32(mlp_in, d_pre, contract_rows)
    d_normed_two = dot_f32(d_pre, w_fc1, contract_cols)
    d_gain2 = jnp.sum(d_normed_two * normed_two, axis=0)
    d_bias2 = jnp.sum(d_normed_two, axis=0)
    d_middle = grad_top + norm_back(normed_two, rate_two, vecs[4], d_normed_two)
    d_scale1 = jnp.sum(d_middle * branch_one, axis=0)
    d_branch1 = (vecs[3] * d_middle).astype(jnp.bfloat16)
    d_proj_bias = jnp.sum(d_branch1.astype(jnp.float32), axis=0)
    d_proj = dot_f32(d_branch1, attended, contract_rows)
    d_attended = dot_f32(d_branch1, w_proj).astype(jnp.bfloat16)
    d_att_heads = lax.all_to_all(
        d_attended.reshape(batches, rows_here, width),
        "tensor", split_axis=2, concat_axis=1, tiled=True,
    )
    shard_fc2 = scatter_matrix(d_fc2)
    shard_fc1 = scatter_matrix(d_fc1)
    shard_proj = scatter_matrix(d_proj)
    d_heads = jnp.concatenate(
        attention_back(qkv, bounds, ids_row, ids_col, att_heads, d_att_heads, lse), axis=2
    )
    d_qkv = lax.all_to_all(d_heads, "tensor", split_axis=1, concat_axis=2, tiled=True)
    d_qkv = d_qkv.reshape(total_rows, tensor_count * 3 * cols_here)
    shard_qkv = scatter_matrix(dot_f32(normed_one_low, d_qkv, contract_rows))
    d_bias_qkv = jnp.sum(d_qkv.astype(jnp.float32), axis=0)
    d_normed_one = dot_f32(d_qkv, w_qkv, contract_cols)
    d_gain1 = jnp.sum(d_normed_one * normed_one, axis=0)
    d_bias1 = jnp.sum(d_normed_one, axis=0)
    input_grad = d_middle + norm_back(normed_one, rate_one, vecs[0], d_normed_one)

    early = [d_proj_bias, d_scale1, d_gain2, d_bias2, d_fc2_bias, d_scale2]
    summed = lax.psum(
        jnp.concatenate([d_gain1, d_bias1] + early + [d_fc1_bias, d_bias_qkv]), everywhere
    )
    place_dp = lax.axis_index("dp")
    place = lax.axis_index("tensor") * dp_count + place_dp
    vec_sums = summed[: 8 * width].reshape(8, width)
    vec_sums = lax.dynamic_slice_in_dim(vec_sums, place_dp * shard_rows, shard_rows, 1)
    fc1_sums = summed[8 * width : 8 * width + hidden]
    grad_fc1_bias = lax.dynamic_slice_in_dim(
        fc1_sums, place * fc1_bias.shape[0], fc1_bias.shape[0], 0
    )
    qkv_sums = summed[8 * width + hidden :].reshape(tensor_count, 3, cols_here)
    qv_sums = jnp.stack([qkv_sums[:, 0].reshape(-1), qkv_sums[:, 2].reshape(-1)])
    grad_qv_bias = lax.dynamic_slice_in_dim(qv_sums, place * short, short, 1)
    shape = tokens.shape
    return (
        block_out.reshape(shape),
        input_grad.astype(jnp.bfloat16).reshape(shape),
        vec_sums[0],
        vec_sums[1],
        jnp.moveaxis(shard_qkv.reshape(shard_rows, 3, cols_here), 1, 0),
        grad_qv_bias,
        shard_proj.T,
        vec_sums[2],
        vec_sums[3],
        vec_sums[4],
        vec_sums[5],
        shard_fc1,
        grad_fc1_bias,
        shard_fc2.T,
        vec_sums[6],
        vec_sums[7],
    )


def solution(mesh):
    in_specs = (
        P(None, ("dp", "tensor"), None),
        P(None, "dp", None),
        P(None, ("dp", "tensor"), None),
        P("dp"),
        P("dp"),
        P(None, "dp", "tensor"),
        P(None, ("tensor", "dp")),
        P("tensor", "dp"),
        P("dp"),
        P("dp"),
        P("dp"),
        P("dp"),
        P("dp", "tensor"),
        P(("tensor", "dp")),
        P("tensor", "dp"),
        P("dp"),
        P("dp"),
    )
    out_specs = (
        P(None, ("dp", "tensor"), None),
        P(None, ("dp", "tensor"), None),
        P("dp"),
        P("dp"),
        P(None, "dp", "tensor"),
        P(None, ("tensor", "dp")),
        P("tensor", "dp"),
        P("dp"),
        P("dp"),
        P("dp"),
        P("dp"),
        P("dp", "tensor"),
        P(("tensor", "dp")),
        P("tensor", "dp"),
        P("dp"),
        P("dp"),
    )
    return jax.shard_map(body, mesh=mesh, in_specs=in_specs, out_specs=out_specs, check_vma=False)
```

time: 2620 us -> 1120 us (0.43)
  waiting for transfers between devices: 1680 us -> 529 us
  matrix products: 518 us -> 123 us
  other arithmetic: 227 us -> 21.1 us
  Pallas kernels: 0 us -> 125 us
  blocking collectives: 89.1 us -> 162 us
  local copies, waits for them, and re-layouts: 61.4 us -> 125 us
    reduce_scatter x13 -> x6, waiting for transfers between devices: 950 us -> 134 us  [the longest x2 86.7 us: scatter_matrix(): lax.psum_scatter(part, 'tensor', scatter_dimension=1, tiled=True)]
    all_gather x12 -> x7, waiting for transfers between devices: 725 us -> 121 us  [the longest x3 121 us: gather_matrix(): part = lax.all_gather(shard, 'tensor', axis=1, tiled=True)]
    dot_general x106 -> x12, matrix products: 509 us -> 123 us  [dot_f32(): lax.dot_general(left, right, dims, preferred_element_type=jnp.float32)]
    all_to_all x0 -> x3, waiting for transfers between devices: none -> 206 us  [the longest x1 105 us: body(): lax.all_to_all(d_heads, 'tensor', split_axis=1, concat_axis=2, tiled=True)]
    pallas_call x0 -> x2, Pallas kernels: none -> 125 us  [the longest x1 69.6 us: attention_back(): pl.pallas_call(backward_kernel, grid_spec=pltpu.PrefetchScalarGridSpec(nu...]
    convert_element_type x36 -> x5, other arithmetic: 112 us -> 10.1 us  [the longest x1 4.36 us: body(): input_grad.astype(jnp.bfloat16).reshape(shape)]
    reduce_sum x38 -> x7, other arithmetic: 83.2 us -> 7.39 us  [the longest x1 4.77 us: body(): d_bias_qkv = jnp.sum(d_qkv.astype(jnp.float32), axis=0)]
    unnamed x7 -> x17, waiting for transfers between devices: 3.23 us -> 68.4 us
  transfers between devices with their start and end apart: 26 -> 18, of which waited for: 22 -> 10; matrix products, arithmetic and copies ran while one was open for 6% -> 19% of each run, Pallas kernels for 0% -> 11%
where the time goes in v1:
time: 1120 us
  waiting for transfers between devices  529 us (47%)
  blocking collectives  162 us (14%)
  local copies, waits for them, and re-layouts  125 us (11%)
  Pallas kernels  125 us (11%)
  matrix products  123 us (11%)
  other arithmetic  21.1 us (2%)
  starting transfers between devices  15.6 us (1%)
  between operations  15.6 us (1%)
    dot_general x12, matrix products, dot_f32(): lax.dot_general(left, right, dims, preferred_element_type=jnp.float32)  123 us
    all_gather x3, waiting for transfers between devices, gather_matrix(): part = lax.all_gather(shard, 'tensor', axis=1, tiled=True)  121 us
    all_to_all x1, waiting for transfers between devices, body(): lax.all_to_all(d_heads, 'tensor', split_axis=1, concat_axis=2, tiled=True)  105 us
    reduce_scatter x2, waiting for transfers between devices, scatter_matrix(): lax.psum_scatter(part, 'tensor', scatter_dimension=1, tiled=True)  86.7 us
    pallas_call x1, Pallas kernels, attention_back(): pl.pallas_call(backward_kernel, grid_spec=pltpu.PrefetchScalarGridSpec(nu...  69.6 us
    unnamed x17, waiting for transfers between devices  68.4 us
    all_to_all x1, waiting for transfers between devices, body(): lax.all_to_all(projected.reshape(batches, rows_here, tensor_count * 3 * c...  65.3 us
    pallas_call x1, Pallas kernels, attention(): pl.pallas_call(forward_kernel, grid_spec=pltpu.PrefetchScalarGridSpec(num...  55.4 us
  transfers between devices with their start and end apart: 18, of which 10 were waited for; matrix products, arithmetic and copies ran while one was open for 19% of the time, Pallas kernels for 11%

profile of v1, /device:TPU:0, one launch (start us, length us, event | category | flops | bytes accessed | tf_op | source)
XLA Modules:
  0.0 1116.3 jit_solution(14591706674202445650)
XLA Ops:
  10.0 47.8 %all-gather.9.cloned.1.call-done = bf16[256,3072]{0,1:T(8,128)(2,1)} async-done(((bf16[256,384]{0,1:T(8,128)(2,1)}), bf16[256,3072]{0,1:T(8,128)(2,1)}) %all-gather.9.cloned.1.call-update) | async-done | bytes 1572880 | tf_op jit(solution)/shard_map/all_gather | solution.py:216
  58.5 34.7 %all_gather.38 = bf16[256,1024]{0,1:T(8,128)(2,1)} all-gather(bf16[256,128]{0,1:T(8,128)(2,1)} %bitcast.164), channel_id=1, replica_groups=mesh['dp'=4,'tensor'=8] {'tensor'}, dimensions={1}, use_global_device_ids=true | all-gather | bytes 589824 | tf_op jit(solution)/shard_map/all_gather | solution.py:216
  93.2 18.8 %all-gather.15.cloned.1.call-done = bf16[256,4096]{1,0:T(8,128)(2,1)} async-done(((bf16[256,512]{1,0:T(8,128)(2,1)}), bf16[256,4096]{1,0:T(8,128)(2,1)}) %all-gather.15.cloned.1.call-update) | async-done | bytes 2097168 | tf_op jit(solution)/shard_map/all_gather | solution.py:216
  114.9 39.4 %all-reduce = bf16[6144]{0:T(1024)(128)(2,1)S(1)} all-reduce(bf16[6144]{0:T(1024)(128)(2,1)S(1)} %dynamic-update-slice), channel_id=2, replica_groups=mesh['dp'=4,'tensor'=8] {'tensor','dp'}, use_global_device_ids=true, to_apply=%add | all-reduce | flops 6144 | bytes 24576
  170.6 12.6 %copy.89 = bf16[2,384,3072]{1,0,2:T(2,128)(2,1)} copy(bf16[2,384,3072]{2,1,0:T(8,128)(2,1)} %bitcast.148) | data formatting | bytes 9437184 | tf_op jit(solution)/shard_map/reshape | solution.py:287
  188.5 54.2 %all-gather.19.cloned.1.call-done = bf16[256,4096]{0,1:T(8,128)(2,1)} async-done(((bf16[256,512]{0,1:T(8,128)(2,1)}), bf16[256,4096]{0,1:T(8,128)(2,1)}) %all-gather.19.cloned.1.call-update) | async-done | bytes 2097168 | tf_op jit(solution)/shard_map/all_gather | solution.py:216
  244.7 65.3 %all-to-all-done = bf16[2,384,3072]{1,0,2:T(2,128)(2,1)} async-done(((bf16[2,384,3072]{1,0,2:T(2,128)(2,1)}), bf16[2,384,3072]{1,0,2:T(2,128)(2,1)}, u32[]{:S(2)}, u32[]{:S(2)}) %all-to-all-start) | async-done | bytes 4718624 | tf_op jit(solution)/shard_map/all_to_all | solution.py:286
  324.0 55.4 %shard_map.288 = (bf16[2,3072,128]{2,1,0:T(8,128)(2,1)S(1)}, f32[2,6,2,512]{3,2,1,0:T(2,128)S(1)}) custom-call(s32[2,6]{1,0:T(2,128)S(1)} %get-tuple-element.156.low_ref, s32[2,6]{1,0:T(2,128)S(1)} %get-tuple-element.155.high_ref, bf16[2,3072,384]{2,1,0:T(8,128)(2,1)S(1)} %bitcast.139, bf16[2,3072,384]{2,1,0:T(8,128)(2,1)S(1)} %bitcast.140, ...), custom_call_target="tpu_custom_call" | custom-call | flops 19327352832 | bytes 4718592 | tf_op jit(solution)/shard_map/pallas_call | solution.py:165
  380.6 13.8 %copy.93 = bf16[2,3072,128]{2,0,1:T(2,128)(2,1)} copy(bf16[2,3072,128]{2,1,0:T(8,128)(2,1)S(1)} %get-tuple-element.21.att_ref) | data formatting | bytes 3145728 | tf_op jit(solution)/shard_map/pallas_call | solution.py:165
  400.4 35.8 %all-to-all-done.1 = bf16[2,3072,128]{2,0,1:T(2,128)(2,1)} async-done(((bf16[2,3072,128]{2,0,1:T(2,128)(2,1)}), bf16[2,3072,128]{2,0,1:T(2,128)(2,1)}, u32[]{:S(2)}, u32[]{:S(2)}) %all-to-all-start.1) | async-done | bytes 1572896 | tf_op jit(solution)/shard_map/all_to_all | solution.py:291
  447.5 15.7 %multiply_convert_fusion = (bf16[768,4096]{1,0:T(8,128)(2,1)}, f32[768,4096]{1,0:T(8,128)}) fusion(f32[4096]{0:T(1024)S(1)} %slice_bitcast_fusion, bf16[1024,4096]{1,0:T(8,128)(2,1)} %all-gather.17.cloned.1.call-done, f32[768,1024]{1,0:T(8,128)} %copy-done.10, f32[1024]{0:T(1024)S(1)} %bitcast.179, f32[1024]{0:T(1024)S(1)} %bitcast.175, ...), kind=kOutput, calls=%fused_computation.8 | convolution fusion | flops 6465257472 | bytes 30439424 | tf_op jit(solution)/shard_map/dot_general | solution.py:20
  463.2 17.0 %convert_reduce_fusion = (f32[4096]{0:T(1024)}, bf16[768,4096]{1,0:T(8,128)(2,1)}) fusion(f32[768,4096]{1,0:T(8,128)} %get-tuple-element.150, f32[4096]{0:T(1024)S(1)} %slice_bitcast_fusion, bf16[768,1024]{1,0:T(8,128)(2,1)S(1)} %copy-done.12, bf16[1024,4096]{0,1:T(8,128)(2,1)} %all-gather.21.cloned.1.call-done), kind=kOutput, calls=%fused_computation.7 | convolution fusion | flops 6483341312 | bytes 28868608 | tf_op jit(solution)/shard_map/dot_general | solution.py:20
  490.8 14.8 %fusion.8 = (f32[1024]{0:T(1024)S(1)}, bf16[768,1024]{1,0:T(8,128)(2,1)}, f32[1024]{0:T(1024)S(1)}, f32[768,1024]{1,0:T(8,128)S(1)}) fusion(bf16[2,384,1024]{2,1,0:T(8,128)(2,1)S(1)} %copy-done.8, f32[1024]{0:T(1024)S(1)} %bitcast.181, f32[768,1024]{1,0:T(8,128)S(1)} %copy-done.11, f32[1024]{0:T(1024)S(1)} %bitcast.167, ...), kind=kOutput, calls=%fused_computation.22 | convolution fusion | flops 6456604672 | bytes 30445568 | tf_op jit(solution)/shard_map/dot_general | solution.py:20
  512.2 11.8 %convolution_convert_fusion = bf16[1024,4096]{1,0:T(8,128)(2,1)} fusion(bf16[768,1024]{1,0:T(8,128)(2,1)S(1)} %copy-done.12, bf16[768,4096]{1,0:T(8,128)(2,1)} %get-tuple-element.149), kind=kOutput, calls=%fused_computation.12 | convolution fusion | flops 6446645248 | bytes 16252928 | tf_op jit(solution)/shard_map/dot_general | solution.py:20
  524.1 12.5 %convolution_convert_fusion.1 = bf16[1024,4096]{1,0:T(8,128)(2,1)} fusion(bf16[768,4096]{1,0:T(8,128)(2,1)} %get-tuple-element.154, f32[768,1024]{1,0:T(8,128)} %copy-done.10, f32[1024]{0:T(1024)S(1)} %bitcast.180, f32[1024]{0:T(1024)S(1)} %bitcast.178, f32[768]{0:T(1024)S(1)} %add_rsqrt_fusion, f32[768]{0:T(1024)S(1)} %broadcast_multiply_fusion.4), kind=kOutput, calls=%fused_computation.13 | convolution fusion | flops 6450577408 | bytes 17840128 | tf_op jit(solution)/shard_map/dot_general | solution.py:20
  546.9 41.7 %all_to_all.66 = bf16[2,384,1024]{1,0,2:T(2,128)(2,1)S(1)} all-to-all(bf16[2,384,1024]{1,0,2:T(2,128)(2,1)S(1)} %copy.95), channel_id=1, replica_groups=mesh['dp'=4,'tensor'=8] {'tensor'}, dimensions={2} | all-to-all | bytes 3145728 | tf_op jit(solution)/shard_map/all_to_all | solution.py:322
  590.4 69.6 %shard_map.289 = (bf16[2,3072,128]{2,1,0:T(8,128)(2,1)S(1)}, bf16[2,3072,128]{2,1,0:T(8,128)(2,1)S(1)}, bf16[2,3072,128]{2,1,0:T(8,128)(2,1)S(1)}) custom-call(s32[2,6]{1,0:T(2,128)S(1)} %get-tuple-element.156.low_ref, s32[2,6]{1,0:T(2,128)S(1)} %get-tuple-element.155.high_ref, bf16[2,3072,384]{2,1,0:T(8,128)(2,1)} %bitcast.136, ...), custom_call_target="tpu_custom_call" | custom-call | flops 48318382080 | bytes 9437184 | tf_op jit(solution)/shard_map/pallas_call | solution.py:195
  660.8 44.7 %copy.99 = bf16[2,3072,384]{2,0,1:T(2,128)(2,1)} copy(bf16[2,3072,384]{2,1,0:T(8,128)(2,1)S(1)} %pad_maximum_fusion) | data formatting | bytes 9437184 | tf_op jit(solution)/shard_map/concatenate | solution.py:329
  714.7 105.4 %all-to-all-done.3 = bf16[2,3072,384]{2,0,1:T(2,128)(2,1)} async-done(((bf16[2,3072,384]{2,0,1:T(2,128)(2,1)}), bf16[2,3072,384]{2,0,1:T(2,128)(2,1)}, u32[]{:S(2)}, u32[]{:S(2)}) %all-to-all-start.3) | async-done | bytes 4718624 | tf_op jit(solution)/shard_map/all_to_all | solution.py:332
  849.7 47.0 %reduce-scatter.13.cloned.1.call-done = bf16[256,3072]{1,0:T(8,128)(2,1)} async-done(((bf16[1024,3072]{1,0:T(8,128)(2,1)}), bf16[256,3072]{1,0:T(8,128)(2,1)}) %reduce-scatter.13.cloned.1.call-update) | async-done | bytes 1572880 | tf_op jit(solution)/shard_map/reduce_scatter | solution.py:221
  904.2 40.7 %psum.7 = f32[15360]{0:T(1024)S(1)} all-reduce(f32[15360]{0:T(1024)S(1)} %constant_dynamic-update-slice_fusion), channel_id=1, replica_groups=mesh['dp'=4,'tensor'=8] {'dp','tensor'}, use_global_device_ids=true, to_apply=%region_20.21 | all-reduce | flops 15360 | bytes 122880 | tf_op jit(solution)/shard_map/psum | solution.py:342
  951.3 17.8 %reduce-scatter.23.cloned.1.call-done = bf16[256,512]{1,0:T(8,128)(2,1)} async-done(((bf16[256,4096]{1,0:T(8,128)(2,1)}), bf16[256,512]{1,0:T(8,128)(2,1)}) %reduce-scatter.23.cloned.1.call-update) | async-done | bytes 262160 | tf_op jit(solution)/shard_map/reduce_scatter | solution.py:222
  971.2 68.9 %reduce-scatter.19.cloned.1.call-done = bf16[256,512]{1,0:T(8,128)(2,1)} async-done(((bf16[256,4096]{1,0:T(8,128)(2,1)}), bf16[256,512]{1,0:T(8,128)(2,1)}) %reduce-scatter.19.cloned.1.call-update) | async-done | bytes 262160 | tf_op jit(solution)/shard_map/reduce_scatter | solution.py:222
  1041.9 65.9 %reduce-scatter.25.cloned.1.call-done = bf16[384,256]{1,0:T(8,128)(2,1)} async-done(((bf16[3072,256]{1,0:T(8,128)(2,1)}), bf16[384,256]{1,0:T(8,128)(2,1)}) %reduce-scatter.25.cloned.1.call-update) | async-done | bytes 196624
  (229 shorter events, 149.5 us)
Async XLA Ops:
  7.2 104.9 %copy-start.34 = (bf16[256]{0:T(256)(128)(2,1)S(1)}, bf16[256]{0:T(256)(128)(2,1)}, u32[]{:S(2)}) copy-start(bf16[256]{0:T(256)(128)(2,1)} %param.26) | copy-start | bytes 1540
  7.2 104.9 %copy-start.35 = (bf16[256]{0:T(256)(128)(2,1)S(1)}, bf16[256]{0:T(256)(128)(2,1)}, u32[]{:S(2)}) copy-start(bf16[256]{0:T(256)(128)(2,1)} %param.27) | copy-start | bytes 1540
  7.2 104.9 %copy-start.36 = (bf16[256]{0:T(256)(128)(2,1)S(1)}, bf16[256]{0:T(256)(128)(2,1)}, u32[]{:S(2)}) copy-start(bf16[256]{0:T(256)(128)(2,1)} %param.28) | copy-start | bytes 1540
  7.2 104.9 %copy-start.37 = (bf16[256]{0:T(256)(128)(2,1)S(1)}, bf16[256]{0:T(256)(128)(2,1)}, u32[]{:S(2)}) copy-start(bf16[256]{0:T(256)(128)(2,1)} %param.32) | copy-start | bytes 1540
  7.3 105.0 %copy-start.38 = (bf16[256]{0:T(256)(128)(2,1)S(1)}, bf16[256]{0:T(256)(128)(2,1)}, u32[]{:S(2)}) copy-start(bf16[256]{0:T(256)(128)(2,1)} %param.33) | copy-start | bytes 1540
  7.3 105.0 %copy-start.4 = (bf16[2,384,1024]{2,1,0:T(8,128)(2,1)S(1)}, bf16[2,384,1024]{2,1,0:T(8,128)(2,1)}, u32[]{:S(2)}) copy-start(bf16[2,384,1024]{2,1,0:T(8,128)(2,1)} %param.17) | copy-start | bytes 4718596
  7.3 50.5 %all-gather.9.cloned.1.call-start = ((), (), s32[]{:S(2)}) async-start(), calls=%async_computation.12 | async-start | bytes 1769472 | tf_op jit(solution)/shard_map/all_gather | solution.py:216
  9.2 102.8 %all-gather.15.cloned.1.call-start = ((), (), s32[]{:S(2)}) async-start(), calls=%async_computation.15 | async-start | bytes 2359296 | tf_op jit(solution)/shard_map/all_gather | solution.py:216
  10.0 151.1 %all-gather.11.cloned.1.call-start = ((), (), s32[]{:S(2)}) async-start(), calls=%async_computation.13 | async-start | bytes 7864320 | tf_op jit(solution)/shard_map/all_gather | solution.py:217
  57.8 184.9 %all-gather.19.cloned.1.call-start = ((), (), s32[]{:S(2)}) async-start(), calls=%async_computation.17 | async-start | bytes 2359296 | tf_op jit(solution)/shard_map/all_gather | solution.py:216
  58.4 381.3 %all-gather.13.cloned.1.call-start = ((), (), s32[]{:S(2)}) async-start(), calls=%async_computation.14 | async-start | bytes 2621440 | tf_op jit(solution)/shard_map/all_gather | solution.py:217
  93.2 354.3 %all-gather.17.cloned.1.call-start = ((), (), s32[]{:S(2)}) async-start(), calls=%async_computation.16 | async-start | bytes 10485760 | tf_op jit(solution)/shard_map/all_gather | solution.py:217
  183.2 126.8 %all-to-all-start = ((bf16[2,384,3072]{1,0,2:T(2,128)(2,1)}), bf16[2,384,3072]{1,0,2:T(2,128)(2,1)}, u32[]{:S(2)}, u32[]{:S(2)}) async-start(bf16[2,384,3072]{1,0,2:T(2,128)(2,1)} %copy.89), calls=%async_computation | async-start | bytes 9437184 | tf_op jit(solution)/shard_map/all_to_all | solution.py:286
  188.2 275.0 %all-gather.21.cloned.1.call-start = ((), (), s32[]{:S(2)}) async-start(), calls=%async_computation.18 | async-start | bytes 10485760 | tf_op jit(solution)/shard_map/all_gather | solution.py:217
  394.4 41.8 %all-to-all-start.1 = ((bf16[2,3072,128]{2,0,1:T(2,128)(2,1)}), bf16[2,3072,128]{2,0,1:T(2,128)(2,1)}, u32[]{:S(2)}, u32[]{:S(2)}) async-start(bf16[2,3072,128]{2,0,1:T(2,128)(2,1)} %copy.93), calls=%async_computation.1 | async-start | bytes 3145728 | tf_op jit(solution)/shard_map/all_to_all | solution.py:291
  398.7 313.4 %reduce-scatter.15.cloned.1.call-start = ((), (), s32[]{:S(2)}) async-start(), calls=%async_computation.20 | async-start | bytes 2621440 | tf_op jit(solution)/shard_map/reduce_scatter | solution.py:221
  512.2 323.5 %reduce-scatter.21.cloned.1.call-start = ((), (), s32[]{:S(2)}) async-start(), calls=%async_computation.23 | async-start | bytes 10485760 | tf_op jit(solution)/shard_map/reduce_scatter | solution.py:221
  524.0 312.4 %reduce-scatter.17.cloned.1.call-start = ((), (), s32[]{:S(2)}) async-start(), calls=%async_computation.21 | async-start | bytes 10485760 | tf_op jit(solution)/shard_map/reduce_scatter | solution.py:221
  705.5 114.6 %all-to-all-start.3 = ((bf16[2,3072,384]{2,0,1:T(2,128)(2,1)}), bf16[2,3072,384]{2,0,1:T(2,128)(2,1)}, u32[]{:S(2)}, u32[]{:S(2)}) async-start(bf16[2,3072,384]{2,0,1:T(2,128)(2,1)} %copy.99), calls=%async_computation.3 | async-start | bytes 9437184 | tf_op jit(solution)/shard_map/all_to_all | solution.py:332
  710.2 127.4 %reduce-scatter.27.cloned.1.call-start = ((), (), s32[]{:S(2)}) async-start(), calls=%async_computation.26 | async-start | bytes 589824
  714.1 182.6 %reduce-scatter.13.cloned.1.call-start = ((), (), s32[]{:S(2)}) async-start(), calls=%async_computation.19 | async-start | bytes 7864320 | tf_op jit(solution)/shard_map/reduce_scatter | solution.py:221
  835.6 133.6 %reduce-scatter.23.cloned.1.call-start = ((), (), s32[]{:S(2)}) async-start(), calls=%async_computation.24 | async-start | bytes 2359296 | tf_op jit(solution)/shard_map/reduce_scatter | solution.py:222
  836.4 203.7 %reduce-scatter.19.cloned.1.call-start = ((), (), s32[]{:S(2)}) async-start(), calls=%async_computation.22 | async-start | bytes 2359296 | tf_op jit(solution)/shard_map/reduce_scatter | solution.py:222
  837.0 270.8 %reduce-scatter.25.cloned.1.call-start = ((), (), s32[]{:S(2)}) async-start(), calls=%async_computation.25 | async-start | bytes 1769472
  (37 other events, 969.3 us)
Sparse Core Ops, SparseCore 0:
  10.9 46.8 all-gather.8
  59.8 52.1 all-gather.14
  113.6 46.6 all-gather.10
  162.2 80.3 all-gather.18
  244.1 44.2 all-gather.12
  289.8 58.3 all-gather.16
  349.7 59.3 all-gather.20
  512.3 30.3 reduce-scatter.14
  545.5 71.7 reduce-scatter.20
  619.7 71.7 reduce-scatter.16
  715.3 121.5 reduce-scatter.26
  839.3 57.3 reduce-scatter.12
  900.7 68.4 reduce-scatter.22
  973.0 67.0 reduce-scatter.18
  1043.7 63.9 reduce-scatter.24
